TPU v7x, 256 devices: a whole 4x4x8 slice. The times are simulated.
256 devices in a mesh: dom: 64 (over y_lo, x, z), edge: 4 (over y_hi, core).
Axes of the slice: x: 4, y: 4 (y_hi: 2, y_lo: 2; y = y_hi * 2 + y_lo), z: 8, core: 2. Of those that a mesh axis runs over, the one named last changes fastest.
Arguments:
- embedding: float32 [16384, 800], P('dom')
- adagrad_state: float32 [16384], P('dom'), may hold values from 0.05 to 1
- relation_table: bfloat16 [128, 800], replicated, may hold values from -4 to 4
- source_row: int32 [2, 64, 1024], P(None, 'dom', 'edge'), may hold values from 0 to 255
- target_row: int32 [2, 64, 1024], P(None, 'dom', 'edge'), may hold values from 0 to 255
- relation_id: int32 [2, 64, 1024], P(None, 'dom', 'edge'), may hold values from 0 to 127
- negative_row: int32 [2, 64, 4, 1024], P(None, 'dom', 'edge'), may hold values from 0 to 255
Outputs:
- new_embedding: float32 [16384, 800], P('dom')
- new_state: float32 [16384], P('dom')
All inputs are finite; a program needn't handle non-finite values.
Results may differ from a plain program's by a relative error of at most 0.008.
Values may be sent and summed in bfloat16 or wider, within the bound.
A program may use at most 64 MiB of HBM per device.

v0:
```python
import jax
import jax.numpy as jnp
from jax import lax
from jax.sharding import PartitionSpec as P

learning_rate = 0.1


def from_behind(value, axis, by):
    length = lax.axis_size(axis)
    return lax.ppermute(value, axis, [(i, (i + by) % length) for i in range(length)])


def complex_times(left, right):
    halfway = left.shape[-1] // 2
    left_real, left_imag = (left[..., :halfway], left[..., halfway:])
    right_real, right_imag = (right[..., :halfway], right[..., halfway:])
    return jnp.concatenate(
        [
            left_real * right_real - left_imag * right_imag,
            left_real * right_imag + left_imag * right_real,
        ],
        axis=-1,
    )


def conjugate_times(grad_value, right):
    halfway = grad_value.shape[-1] // 2
    grad_real, grad_imag = (grad_value[..., :halfway], grad_value[..., halfway:])
    right_real, right_imag = (right[..., :halfway], right[..., halfway:])
    return jnp.concatenate(
        [
            grad_real * right_real + grad_imag * right_imag,
            grad_imag * right_real - grad_real * right_imag,
        ],
        axis=-1,
    )


def group_terms(sources, targets, negatives, relations):
    product = complex_times(sources.astype(jnp.float32), relations).astype(jnp.bfloat16)
    product_wide = product.astype(jnp.float32)
    targets_wide = targets.astype(jnp.float32)
    positive = jnp.sum(product_wide * targets_wide, axis=1)
    negative = lax.dot_general(
        product, negatives, (((1,), (1,)), ((), ())), preferred_element_type=jnp.float32
    )
    highest = jnp.maximum(jnp.max(negative, axis=1), positive)
    expo_neg = jnp.exp(negative - highest[:, None])
    expo_pos = jnp.exp(positive - highest)
    total = jnp.sum(expo_neg, axis=1) + expo_pos
    weights = (expo_neg / total[:, None]).astype(jnp.bfloat16)
    pull = expo_pos / total - 1.0
    grad_product = pull[:, None] * targets_wide + jnp.dot(
        weights, negatives, preferred_element_type=jnp.float32
    )
    grad_sources = conjugate_times(grad_product, relations)
    grad_targets = pull[:, None] * product_wide
    grad_negatives = lax.dot_general(
        weights, product, (((0,), (0,)), ((), ())), preferred_element_type=jnp.float32
    )
    return (grad_sources, grad_targets, grad_negatives)


def bucket_gradients(own_block, partner_block, relations, source_row, target_row, negative_row):
    groups = negative_row.shape[0]
    group_size = source_row.shape[0] // groups
    feature_width = own_block.shape[1]
    row_count = own_block.shape[0]
    sources = jnp.take(own_block, source_row, axis=0).reshape(groups, group_size, feature_width)
    targets = jnp.take(partner_block, target_row, axis=0).reshape(groups, group_size, feature_width)
    relations = relations.reshape(groups, group_size, feature_width)

    def per_group(group_items):
        source_part, target_part, relation_part, negative_index = group_items
        negatives = jnp.take(partner_block, negative_index, axis=0)
        return group_terms(source_part, target_part, negatives, relation_part)

    grad_sources, grad_targets, grad_negatives = lax.map(
        per_group, (sources, targets, relations, negative_row)
    )
    grad_source = jax.ops.segment_sum(
        grad_sources.reshape(-1, feature_width), source_row, num_segments=row_count
    )
    grad_target = jax.ops.segment_sum(
        grad_targets.reshape(-1, feature_width), target_row, num_segments=row_count
    )
    grad_target = grad_target + jax.ops.segment_sum(
        grad_negatives.reshape(-1, feature_width), negative_row.reshape(-1), num_segments=row_count
    )
    return (grad_source, grad_target)


def relation_lookup(relation_table, relation_id):
    codes = jnp.arange(relation_table.shape[0], dtype=jnp.int32)
    picks = (relation_id[:, None] == codes[None, :]).astype(jnp.bfloat16)
    return jnp.dot(picks, relation_table, preferred_element_type=jnp.float32)


def adagrad_step(weights, state, gradient):
    new_state = state + jnp.mean(gradient * gradient, axis=1)
    return (weights - learning_rate * gradient / jnp.sqrt(new_state)[:, None], new_state)


def body(
    embedding, adagrad_state, relation_table, source_row, target_row, relation_id, negative_row
):
    weights, state = (embedding, adagrad_state)
    rounds_count = source_row.shape[0]
    for round_index in range(rounds_count):
        own_block = weights.astype(jnp.bfloat16)
        partner_block = from_behind(own_block, "dom", round_index + 1)
        relations = relation_lookup(relation_table, relation_id[round_index, 0])
        grad_source, grad_target = bucket_gradients(
            own_block,
            partner_block,
            relations,
            source_row[round_index, 0],
            target_row[round_index, 0],
            negative_row[round_index, 0],
        )
        returned = from_behind(grad_target, "dom", -(round_index + 1))
        gradient = lax.psum(grad_source + returned, "edge")
        weights, state = adagrad_step(weights, state, gradient)
    return (weights, state)


def solution(mesh):
    in_specs = (
        P("dom", None),
        P("dom"),
        P(),
        P(None, "dom", "edge"),
        P(None, "dom", "edge"),
        P(None, "dom", "edge"),
        P(None, "dom", "edge", None),
    )
    out_specs = (P("dom", None), P("dom"))
    return jax.shard_map(body, mesh=mesh, in_specs=in_specs, out_specs=out_specs, check_vma=False)
```

profile of v0, /device:TPU:33, one launch (start us, length us, event | category | flops | bytes accessed | tf_op | source)
XLA Modules:
  0.0 305.9 jit_solution(11078831381754638085)
XLA Ops:
  12.7 7.6 %collective-permute-done = bf16[256,800]{1,0:T(8,128)(2,1)S(1)} collective-permute-done((bf16[256,800]{1,0:T(8,128)(2,1)S(1)}, bf16[256,800]{1,0:T(8,128)(2,1)S(1)}, u32[]{:S(2)}, u32[]{:S(2)}) %collective-permute-start) | collective-permute-done | bytes 409632 | tf_op jit(solution)/shard_map/ppermute | solution.py:11
  23.6 5.3 %gather_fusion.2 = bf16[1024,800]{1,0:T(8,128)(2,1)} fusion(bf16[256,800]{1,0:T(8,128)(2,1)S(1)} %collective-permute-done, s32[1024]{0:T(1024)S(1)} %fusion.22), kind=kCustom, calls=%fused_computation.1.clone | custom fusion | bytes 3280896 | tf_op jit(solution)/shard_map/while/body/eval_jaxpr/jit(_take)/gather | solution.py:76
  28.9 2.6 fusion.39
  31.8 2.7 fusion.32
  35.8 10.4 %scatter_custom_fusion.1 = f32[256,800]{1,0:T(8,128)S(1)} fusion(s32[1024]{0:T(1024)S(1)} %bitcast.15, f32[1024,800]{1,0:T(8,128)} %fusion.32, f32[]{:T(128)} %constant.70.clone.1), kind=kCustom, calls=%fused_computation.44 | custom fusion | flops 819200 | bytes 819712 | tf_op jit(solution)/shard_map/scatter-add | solution.py:88
  46.3 4.2 %scatter_custom_fusion = f32[256,800]{1,0:T(8,128)} fusion(s32[256]{0:T(256)S(1)} %bitcast.29, f32[256,800]{1,0:T(8,128)} %copy.32, f32[]{:T(128)} %constant.70.clone.1), kind=kCustom, calls=%fused_computation.46 | custom fusion | flops 204800 | bytes 819712 | tf_op jit(solution)/shard_map/scatter-add | solution.py:85
  52.8 2.3 copy.34
  55.1 7.5 %collective-permute-start.1 = (f32[256,800]{0,1:T(8,128)}, f32[256,800]{0,1:T(8,128)}, u32[]{:S(2)}, u32[]{:S(2)}) collective-permute-start(f32[256,800]{0,1:T(8,128)} %copy.34), channel_id=1, source_target_pairs={{0,252},{4,0},{8,4},{12,8},{16,12},{20,16},{24,20},{28,24},{32,28}... | collective-permute-start | bytes 2457608 | tf_op jit(solution)/shard_map/ppermute | solution.py:11
  62.6 3.0 fusion.3
  66.1 13.2 %collective-permute-done.1 = f32[256,800]{0,1:T(8,128)} collective-permute-done((f32[256,800]{0,1:T(8,128)}, f32[256,800]{0,1:T(8,128)}, u32[]{:S(2)}, u32[]{:S(2)}) %collective-permute-start.1) | collective-permute-done | bytes 819232 | tf_op jit(solution)/shard_map/ppermute | solution.py:11
  80.7 3.0 scatter_fusion
  85.1 51.2 %all-reduce.3.cloned.1.call-done = f32[256,800]{1,0:T(8,128)} async-done(((f32[256,800]{1,0:T(8,128)}), f32[256,800]{1,0:T(8,128)}) %all-reduce.3.cloned.1.call-update) | async-done | bytes 819216 | tf_op jit(solution)/shard_map/psum | solution.py:123
  144.8 21.7 %collective-permute-done.2 = bf16[256,800]{1,0:T(8,128)(2,1)S(1)} collective-permute-done((bf16[256,800]{1,0:T(8,128)(2,1)S(1)}, bf16[256,800]{1,0:T(8,128)(2,1)S(1)}, u32[]{:S(2)}, u32[]{:S(2)}) %collective-permute-start.2) | collective-permute-done | bytes 409632 | tf_op jit(solution)/shard_map/ppermute | solution.py:11
  169.8 5.3 %gather_fusion.5 = bf16[1024,800]{1,0:T(8,128)(2,1)} fusion(bf16[256,800]{1,0:T(8,128)(2,1)S(1)} %collective-permute-done.2, s32[1024]{0:T(1024)S(1)} %fusion.23), kind=kCustom, calls=%fused_computation.5.clone | custom fusion | bytes 3280896 | tf_op jit(solution)/shard_map/while/body/eval_jaxpr/jit(_take)/gather | solution.py:76
  175.1 2.6 fusion.40
  178.7 2.7 fusion.31
  181.4 10.4 %scatter_custom_fusion.4 = f32[256,800]{1,0:T(8,128)S(1)} fusion(s32[1024]{0:T(1024)S(1)} %bitcast.12, f32[1024,800]{1,0:T(8,128)} %fusion.31, f32[]{:T(128)} %constant.70.clone.1), kind=kCustom, calls=%fused_computation.40 | custom fusion | flops 819200 | bytes 819712 | tf_op jit(solution)/shard_map/scatter-add | solution.py:88
  192.8 2.4 copy.40
  195.1 4.2 %scatter_custom_fusion.3 = f32[256,800]{1,0:T(8,128)} fusion(s32[256]{0:T(256)S(1)} %bitcast.26, f32[256,800]{1,0:T(8,128)} %copy.40, f32[]{:T(128)} %constant.70.clone.1), kind=kCustom, calls=%fused_computation.42 | custom fusion | flops 204800 | bytes 819712 | tf_op jit(solution)/shard_map/scatter-add | solution.py:85
  199.4 2.4 add.112
  204.6 2.9 fusion.5
  208.0 32.1 %collective-permute-done.3 = f32[256,800]{0,1:T(8,128)} collective-permute-done((f32[256,800]{0,1:T(8,128)}, f32[256,800]{0,1:T(8,128)}, u32[]{:S(2)}, u32[]{:S(2)}) %collective-permute-start.3) | collective-permute-done | bytes 819232 | tf_op jit(solution)/shard_map/ppermute | solution.py:11
  241.6 3.0 scatter_fusion.1
  245.6 48.9 %all-reduce.5.cloned.1.call-done = f32[256,800]{1,0:T(8,128)} async-done(((f32[256,800]{1,0:T(8,128)}), f32[256,800]{1,0:T(8,128)}) %all-reduce.5.cloned.1.call-update) | async-done | bytes 819216 | tf_op jit(solution)/shard_map/psum | solution.py:123
  (97 shorter events, 39.8 us)
Async XLA Ops:
  7.2 5.0 %copy-start = (bf16[128,800]{0,1:T(8,128)(2,1)S(1)}, bf16[128,800]{0,1:T(8,128)(2,1)}, u32[]{:S(2)}) copy-start(bf16[128,800]{0,1:T(8,128)(2,1)} %param.13) | copy-start | bytes 614404
  7.2 3.3 %copy-start.10 = (s32[2,1,256]{2,1,0:T(1,128)S(1)}, s32[2,1,256]{2,1,0:T(1,128)}, u32[]{:S(2)}) copy-start(s32[2,1,256]{2,1,0:T(1,128)} %param.14) | copy-start | bytes 6148
  7.2 3.3 %copy-start.11 = (s32[2,1,256]{2,1,0:T(1,128)S(1)}, s32[2,1,256]{2,1,0:T(1,128)}, u32[]{:S(2)}) copy-start(s32[2,1,256]{2,1,0:T(1,128)} %param.15) | copy-start | bytes 6148
  7.2 3.4 %copy-start.8 = (s32[2,1,1,1024]{3,2,1,0:T(1,128)S(1)}, s32[2,1,1,1024]{3,2,1,0:T(1,128)}, u32[]{:S(2)}) copy-start(s32[2,1,1,1024]{3,2,1,0:T(1,128)} %param.17) | copy-start | bytes 24580
  7.2 129.1 %all-reduce.3.cloned.1.call-start = ((), (), s32[]{:S(2)}) async-start(), calls=%async_computation | async-start | bytes 1835008 | tf_op jit(solution)/shard_map/psum | solution.py:123
  8.8 11.5 %collective-permute-start = (bf16[256,800]{1,0:T(8,128)(2,1)S(1)}, bf16[256,800]{1,0:T(8,128)(2,1)S(1)}, u32[]{:S(2)}, u32[]{:S(2)}) collective-permute-start(bf16[256,800]{1,0:T(8,128)(2,1)S(1)} %convert_element_type.48), channel_id=1, source_target_pairs={{0,4},{4,8},{8,12},{12,16},{16,20},{20,24},{24,28},{28,32},{32,36}... | collective-permute-start | bytes 1228808 | tf_op jit(solution)/shard_map/ppermute | solution.py:11
  10.7 1.4 copy-start.12
  31.4 3.1 %copy-start.7 = (f32[256,1024]{1,0:T(8,128)}, f32[256,1024]{1,0:T(8,128)S(1)}, u32[]{:S(2)}) copy-start(f32[256,1024]{1,0:T(8,128)S(1)} %get-tuple-element.87) | copy-start | bytes 3145732
  50.5 12.2 %copy-start.5 = (bf16[256,800]{0,1:T(8,128)(2,1)S(1)}, bf16[256,800]{0,1:T(8,128)(2,1)}, u32[]{:S(2)}) copy-start(bf16[256,800]{0,1:T(8,128)(2,1)} %copy.31) | copy-start | bytes 1228804
  55.1 24.1 %collective-permute-start.1 = (f32[256,800]{0,1:T(8,128)}, f32[256,800]{0,1:T(8,128)}, u32[]{:S(2)}, u32[]{:S(2)}) collective-permute-start(f32[256,800]{0,1:T(8,128)} %copy.34), channel_id=1, source_target_pairs={{0,252},{4,0},{8,4},{12,8},{16,12},{20,16},{24,20},{28,24},{32,28}... | collective-permute-start | bytes 2457608 | tf_op jit(solution)/shard_map/ppermute | solution.py:11
  83.7 0.9 copy-start.1
  83.7 53.9 %copy-start.9 = (f32[256]{0:T(256)S(1)}, f32[256]{0:T(256)}, u32[]{:S(2)}) copy-start(f32[256]{0:T(256)} %param.12) | copy-start | bytes 3076
  84.6 209.8 %all-reduce.5.cloned.1.call-start = ((), (), s32[]{:S(2)}) async-start(), calls=%async_computation.1 | async-start | bytes 1835008 | tf_op jit(solution)/shard_map/psum | solution.py:123
  139.1 27.4 %collective-permute-start.2 = (bf16[256,800]{1,0:T(8,128)(2,1)S(1)}, bf16[256,800]{1,0:T(8,128)(2,1)S(1)}, u32[]{:S(2)}, u32[]{:S(2)}) collective-permute-start(bf16[256,800]{1,0:T(8,128)(2,1)S(1)} %fusion.33), channel_id=1, source_target_pairs={{0,8},{4,12},{8,16},{12,20},{16,24},{20,28},{24,32},{28,36},{32,40... | collective-permute-start | bytes 1228808 | tf_op jit(solution)/shard_map/ppermute | solution.py:11
  177.7 1.0 copy-start.6
  199.4 5.2 %copy-start.4 = (bf16[256,800]{0,1:T(8,128)(2,1)S(1)}, bf16[256,800]{0,1:T(8,128)(2,1)}, u32[]{:S(2)}) copy-start(bf16[256,800]{0,1:T(8,128)(2,1)} %copy.39) | copy-start | bytes 1228804
  204.1 36.1 %collective-permute-start.3 = (f32[256,800]{0,1:T(8,128)}, f32[256,800]{0,1:T(8,128)}, u32[]{:S(2)}, u32[]{:S(2)}) collective-permute-start(f32[256,800]{0,1:T(8,128)} %copy.42), channel_id=1, source_target_pairs={{0,248},{4,252},{8,0},{12,4},{16,8},{20,12},{24,16},{28,20},{32,24... | collective-permute-start | bytes 2457608 | tf_op jit(solution)/shard_map/ppermute | solution.py:11
  244.6 1.0 copy-start.2
  244.6 51.7 %copy-start.3 = (f32[256,800]{1,0:T(8,128)S(1)}, f32[256,800]{1,0:T(8,128)}, u32[]{:S(2)}) copy-start(f32[256,800]{1,0:T(8,128)} %all-reduce.3.cloned.1.call-done) | copy-start | bytes 2457604
Sparse Core Ops, SparseCore 0:
  84.8 51.5 all-reduce.2
  245.7 48.6 all-reduce.4
where the time goes:
time: 308 us; the launch traced here: 306 us
  waiting for transfers between devices  175 us (57%)
  other arithmetic  52 us (17%)
  local copies, waits for them, and re-layouts  35.4 us (11%)
  matrix products  17.1 us (6%)
  between operations  14.5 us (5%)
  starting transfers between devices  12.1 us (4%)
    psum x2, waiting for transfers between devices, body(): gradient = lax.psum(grad_source + returned, 'edge')  100 us
    ppermute x4, waiting for transfers between devices, from_behind(): lax.ppermute(value, axis, [(i, (i + by) % length) for i in range(length)])  74.6 us
    scatter-add x2, other arithmetic, bucket_gradients(): jax.ops.segment_sum(grad_negatives.reshape(-1, feature_width), negative_r...  20.9 us
    ppermute x4, starting transfers between devices, from_behind(): lax.ppermute(value, axis, [(i, (i + by) % length) for i in range(length)])  12 us
    gather x2, local copies, waits for them, and re-layouts, per_group(): negatives = jnp.take(partner_block, negative_index, axis=0)  10.5 us
    scatter-add x2, other arithmetic, bucket_gradients(): jax.ops.segment_sum(grad_targets.reshape(-1, feature_width), target_row,...  8.44 us
  transfers between devices with their start and end apart: 6, of which 6 were waited for; matrix products, arithmetic and copies ran while one was open for 4% of the time, Pallas kernels for 0%

commit v1 on v0

v1 whole, which is shorter than its diff:
```python
import functools

import jax
import jax.numpy as jnp
from jax import lax
from jax.experimental import pallas as pl
from jax.experimental.pallas import tpu as pltpu
from jax.sharding import PartitionSpec as P

MESH = pl.DeviceIdType.MESH
F32 = jnp.float32
BF16 = jnp.bfloat16

learning_rate = 0.1
ROWS = 256
HALF = 128
GROUPS = 4
E = 256
WIDE = 896
FULL = 1024


def lanes(shape):
    return lax.broadcasted_iota(jnp.int32, shape, 1)


def arrange(tiles):
    lane = lanes(tiles[0].shape)
    moved = [pltpu.roll(t, 112, 1) for t in tiles[3:7]]
    imag = [jnp.where(lane < 112, moved[j], moved[j + 1]) for j in range(3)]
    tail = jnp.where(lane < 16, tiles[3], jnp.where(lane < 32, tiles[6], 0.0))
    return tiles[:3] + imag + [tail]


def swapped(tail):
    lane = lanes(tail.shape)
    return jnp.where(
        lane < 16, pltpu.roll(tail, 112, 1), jnp.where(lane < 32, pltpu.roll(tail, 16, 1), 0.0)
    )


def natural_tiles(ref, rows):
    parts = [ref[rows, 128 * j : 128 * (j + 1)].astype(F32) for j in range(6)]
    last = ref[rows, 768:800].astype(F32)
    return parts + [jnp.concatenate([last, jnp.zeros((last.shape[0], 96), F32)], axis=1)]


def dot(a, b, ca, cb):
    return lax.dot_general(a, b, (((ca,), (cb,)), ((), ())), preferred_element_type=F32)


def kernel(
    n_dom,
    emb, state, rel, src, tgt, rid, neg,
    out_w, out_s,
    nat, statev, relv, srcv, tgtv, ridv, negv,
    pack, idx, buf, w, scol, rtab, r, q, ots, lc, gt, gs, xs, xr,
    load_sem, row_send, row_recv, idx_send, idx_recv, x_send, x_recv,
):
    d = lax.axis_index("dom")
    e = lax.axis_index("edge")
    core = lax.rem(e, 2)
    plane = e - core
    sibling = plane + (1 - core)
    up = [lax.rem(d + k + 1, n_dom) for k in range(2)]
    down = [lax.rem(d + n_dom - k - 1, n_dom) for k in range(2)]

    barrier = pltpu.get_barrier_semaphore()

    def tell(dom, edge):
        pl.semaphore_signal(barrier, inc=1, device_id=(dom, edge), device_id_type=MESH)

    @pl.when(core == 0)
    def _():
        for k in range(2):
            tell(down[k], plane)
            tell(down[k], plane + 1)
        tell(d, sibling)
        tell(d, 2 - plane)
        tell(d, 3 - plane)

    @pl.when(core == 1)
    def _():
        for k in range(2):
            for g in range(GROUPS):
                tell(up[k], g)
        tell(d, sibling)

    loads = [
        pltpu.make_async_copy(a, b, load_sem.at[i])
        for i, (a, b) in enumerate(
            zip((src, tgt, rid, neg, emb, state, rel), (srcv, tgtv, ridv, negv, nat, statev, relv))
        )
    ]
    for c in loads:
        c.start()
    for c in loads[:4]:
        c.wait()
    for k in range(2):
        pack[k, 0:1, :] = srcv[k]
        pack[k, 1:2, :] = tgtv[k]
        pack[k, 2:3, :] = ridv[k]
        for j in range(4):
            pack[k, 3 + j : 4 + j, :] = negv[k, 0, :, 256 * j : 256 * (j + 1)]

    @pl.when(core == 0)
    def _():
        for k in range(2):
            idx[k, e] = pack[k]

    for c in loads[4:]:
        c.wait()
    tiles = arrange(natural_tiles(nat, slice(None)))
    for j in range(7):
        w[:, 128 * j : 128 * (j + 1)] = tiles[j]
        buf[0, core, :, 128 * j : 128 * (j + 1)] = tiles[j].astype(BF16)
    buf[0, core, :, WIDE:FULL] = swapped(tiles[6]).astype(BF16)

    pl.semaphore_wait(barrier, 8)

    def idx_copy(k, j, group, dom, edge):
        return pltpu.make_async_remote_copy(
            src_ref=pack.at[k],
            dst_ref=idx.at[k, group],
            send_sem=idx_send.at[k, j],
            recv_sem=idx_recv.at[k, group],
            device_id=(dom, edge),
            device_id_type=MESH,
        )

    def idx_sends(k, act):
        for h in range(2):
            pl.when(e != 2 * h)(lambda h=h: act(idx_copy(k, h, e, d, 2 * h)))
            act(idx_copy(k, 2 + h, e, down[k], 2 * h + 1))

    def idx_waits(k):
        for g in range(GROUPS):
            pl.when(e != g + 4 * core)(lambda g=g: idx_copy(k, 0, g, d, sibling).wait_recv())

    mine = pl.ds(pl.multiple_of(core * HALF, HALF), HALF)
    other = pl.ds(pl.multiple_of((1 - core) * HALF, HALF), HALF)

    def row_copy(k, way):
        return pltpu.make_async_remote_copy(
            src_ref=buf.at[k, core, mine, pl.ds(0, WIDE)],
            dst_ref=buf.at[k, 1 - way, mine, pl.ds(0, WIDE)],
            send_sem=row_send.at[k, way],
            recv_sem=row_recv.at[k, core],
            device_id=((up[k], plane), (down[k], plane + 1))[way],
            device_id_type=MESH,
        )

    def row_arrival(k, half):
        part = pl.ds(half * HALF, HALF)
        return pltpu.make_async_remote_copy(
            src_ref=buf.at[k, core, part, pl.ds(0, WIDE)],
            dst_ref=buf.at[k, 1 - core, part, pl.ds(0, WIDE)],
            send_sem=row_send.at[k, half],
            recv_sem=row_recv.at[k, half],
            device_id=(d, sibling),
            device_id_type=MESH,
        )

    def x_copy(k, j):
        part = (other, mine)[j]
        return pltpu.make_async_remote_copy(
            src_ref=xs.at[k, part],
            dst_ref=xr.at[k, part],
            send_sem=x_send.at[k, j],
            recv_sem=x_recv.at[k, j],
            device_id=(d, sibling),
            device_id_type=MESH,
        )

    idx_sends(0, lambda c: c.start())
    row_copy(0, 0).start()
    row_copy(0, 1).start()
    idx_sends(1, lambda c: c.start())

    tiles = arrange(natural_tiles(relv, slice(None)))
    lane = lanes((128, 128))
    swap = swapped(tiles[6])
    for j in range(6):
        rtab[:, 128 * j : 128 * (j + 1)] = tiles[j].astype(BF16)
    rtab[:, 768:896] = jnp.where(lane < 16, tiles[6], swap).astype(BF16)
    rtab[:, 896:1024] = jnp.where(lane < 16, -swap, tiles[6]).astype(BF16)
    eye = lax.broadcasted_iota(jnp.int32, (ROWS, ROWS), 0) == lanes((ROWS, ROWS))
    row = jnp.reshape(statev[...], (1, ROWS))
    scol[...] = jnp.sum(jnp.where(eye, row, 0.0), axis=1, keepdims=True)

    def prepare(k):
        idx_waits(k)
        at = lax.broadcasted_iota(jnp.int32, (ROWS, E), 0)
        for g in range(GROUPS):
            cols = slice(g * E, (g + 1) * E)
            ots[:, cols] = jnp.where(at == idx[k, g, 0:1, :], 1.0, 0.0).astype(BF16)
            count = jnp.zeros((ROWS, E), F32)
            for j in range(4):
                count += jnp.where(at == idx[k, g, 3 + j : 4 + j, :], 1.0, 0.0)
            lc[:, g : g + 1] = jnp.log(jnp.sum(count, axis=1, keepdims=True))
            kind = jnp.where(at[:HALF] == idx[k, g, 2:3, :], 1.0, 0.0).astype(BF16)
            r[cols, :] = dot(kind, rtab[...], 0, 0).astype(BF16)

    def products(k):
        for g in range(GROUPS):
            cols = slice(g * E, (g + 1) * E)
            s = dot(ots[:, cols], buf[k, 0], 0, 0)
            rr = r[cols, :].astype(F32)
            re = s[:, :384] * rr[:, :384] - s[:, 384:768] * rr[:, 384:768]
            im = s[:, :384] * rr[:, 384:768] + s[:, 384:768] * rr[:, :384]
            tail = s[:, 768:896] * rr[:, 768:896] + s[:, 896:] * rr[:, 896:]
            q[cols, 0:384] = re.astype(BF16)
            q[cols, 384:768] = im.astype(BF16)
            q[cols, 768:896] = tail.astype(BF16)

    def pulls(k):
        at = lax.broadcasted_iota(jnp.int32, (ROWS, E), 0)
        for g in range(GROUPS):
            cols = slice(g * E, (g + 1) * E)
            score = dot(buf[k, 1, :, 0:WIDE], q[cols, :], 1, 1)
            hit = at == idx[k, g, 1:2, :]
            pos = jnp.sum(jnp.where(hit, score, 0.0), axis=0, keepdims=True)
            z = score + lc[:, g : g + 1]
            top = jnp.maximum(jnp.max(z, axis=0, keepdims=True), pos)
            ez = jnp.exp(z - top)
            ep = jnp.exp(pos - top)
            inv = 1.0 / (jnp.sum(ez, axis=0, keepdims=True) + ep)
            pull = ep * inv - 1.0
            gt[:, cols] = (ez * inv + jnp.where(hit, pull, 0.0)).astype(BF16)

    def source_terms(k):
        for g in range(GROUPS):
            cols = slice(g * E, (g + 1) * E)
            gq = dot(gt[:, cols], buf[k, 1], 0, 0)
            rr = r[cols, :].astype(F32)
            re = gq[:, :384] * rr[:, :384] + gq[:, 384:768] * rr[:, 384:768]
            im = gq[:, 384:768] * rr[:, :384] - gq[:, :384] * rr[:, 384:768]
            tail = gq[:, 768:896] * rr[:, 768:896] - gq[:, 896:] * rr[:, 896:]
            gs[cols, 0:384] = re.astype(BF16)
            gs[cols, 384:768] = im.astype(BF16)
            gs[cols, 768:896] = tail.astype(BF16)

    def update(k, part, last):
        g = xs[k, part].astype(F32) + xr[k, part].astype(F32)
        new_s = scol[part] + jnp.sum(g * g, axis=1, keepdims=True) * (1.0 / 800.0)
        new_w = w[part] - g * (learning_rate * lax.rsqrt(new_s))
        scol[part] = new_s
        if not last:
            w[part] = new_w
            buf[1, core, part, 0:WIDE] = new_w.astype(BF16)
            buf[1, core, part, WIDE:FULL] = swapped(new_w[:, 768:896]).astype(BF16)
        else:
            t = [new_w[:, 128 * j : 128 * (j + 1)] for j in range(7)]
            moved = [pltpu.roll(v, 16, 1) for v in t[3:6]]
            lane = lanes(t[0].shape)
            for j in range(3):
                out_w[part, 128 * j : 128 * (j + 1)] = t[j]
            out_w[part, 384:512] = jnp.where(lane < 16, t[6], moved[0])
            out_w[part, 512:640] = jnp.where(lane < 16, moved[0], moved[1])
            out_w[part, 640:768] = jnp.where(lane < 16, moved[1], moved[2])
            out_w[part, 768:800] = jnp.where(lane < 16, moved[2], t[6])[:, :32]

    for k in range(2):
        prepare(k)
        pl.when(core == 0)(lambda k=k: products(k))
        for half in range(2):
            row_arrival(k, half).wait_recv()
        tail = buf[k, 1 - core, :, 768:896].astype(F32)
        buf[k, 1 - core, :, WIDE:FULL] = swapped(tail).astype(BF16)
        pl.when(core == 1)(lambda k=k: products(k))
        pulls(k)
        pl.when(core == 0)(lambda k=k: source_terms(k))
        for j, part in enumerate((other, mine)):

            @pl.when(core == 0)
            def _():
                xs[k, part] = dot(ots[part, :], gs[...], 1, 0).astype(BF16)

            @pl.when(core == 1)
            def _():
                xs[k, part] = dot(gt[part, :], q[...], 1, 0).astype(BF16)

            x_copy(k, j).start()
        x_copy(k, 0).wait_recv()
        update(k, mine, k == 1)
        if k == 0:
            row_copy(1, 0).start()
            row_copy(1, 1).start()
        x_copy(k, 1).wait_recv()
        update(k, other, k == 1)

    out_s[...] = jnp.reshape(jnp.sum(jnp.where(eye, scol[...], 0.0), axis=0, keepdims=True), (ROWS,))
    for k in range(2):
        idx_sends(k, lambda c: c.wait_send())
        for j in range(2):
            row_copy(k, j).wait_send()
            x_copy(k, j).wait_send()


def solution(mesh):
    n_dom = mesh.shape["dom"]

    def body(embedding, adagrad_state, relation_table, source_row, target_row, relation_id, negative_row):
        any_space = pl.BlockSpec(memory_space=pl.ANY)
        vmem = pl.BlockSpec(memory_space=pltpu.VMEM)
        dma = pltpu.SemaphoreType.DMA
        return pl.pallas_call(
            functools.partial(kernel, n_dom),
            out_shape=(
                jax.ShapeDtypeStruct(embedding.shape, F32),
                jax.ShapeDtypeStruct(adagrad_state.shape, F32),
            ),
            in_specs=[any_space] * 7,
            out_specs=(vmem, vmem),
            scratch_shapes=[
                pltpu.VMEM(embedding.shape, F32),
                pltpu.VMEM(adagrad_state.shape, F32),
                pltpu.VMEM(relation_table.shape, BF16),
                pltpu.VMEM(source_row.shape, jnp.int32),
                pltpu.VMEM(target_row.shape, jnp.int32),
                pltpu.VMEM(relation_id.shape, jnp.int32),
                pltpu.VMEM(negative_row.shape, jnp.int32),
                pltpu.VMEM((2, 8, E), jnp.int32),
                pltpu.VMEM((2, GROUPS, 8, E), jnp.int32),
                pltpu.VMEM((2, 2, ROWS, FULL), BF16),
                pltpu.VMEM((ROWS, WIDE), F32),
                pltpu.VMEM((ROWS, 1), F32),
                pltpu.VMEM((128, FULL), BF16),
                pltpu.VMEM((GROUPS * E, FULL), BF16),
                pltpu.VMEM((GROUPS * E, WIDE), BF16),
                pltpu.VMEM((ROWS, GROUPS * E), BF16),
                pltpu.VMEM((ROWS, GROUPS), F32),
                pltpu.VMEM((ROWS, GROUPS * E), BF16),
                pltpu.VMEM((GROUPS * E, WIDE), BF16),
                pltpu.VMEM((2, ROWS, WIDE), BF16),
                pltpu.VMEM((2, ROWS, WIDE), BF16),
                dma((7,)),
                dma((2, 2)),
                dma((2, 2)),
                dma((2, 4)),
                dma((2, 4)),
                dma((2, 2)),
                dma((2, 2)),
            ],
            compiler_params=pltpu.CompilerParams(
                collective_id=0, has_side_effects=True, vmem_limit_bytes=48 * 2**20
            ),
        )(embedding, adagrad_state, relation_table, source_row, target_row, relation_id, negative_row)

    in_specs = (
        P("dom", None),
        P("dom"),
        P(),
        P(None, "dom", "edge"),
        P(None, "dom", "edge"),
        P(None, "dom", "edge"),
        P(None, "dom", "edge", None),
    )
    out_specs = (P("dom", None), P("dom"))
    return jax.shard_map(body, mesh=mesh, in_specs=in_specs, out_specs=out_specs, check_vma=False)
```

time: 308 us -> 46.4 us (0.15)
  waiting for transfers between devices: 175 us -> 0 us
  other arithmetic: 52 us -> 0 us
  Pallas kernels: 0 us -> 41.2 us
  local copies, waits for them, and re-layouts: 35.4 us -> 4.31 us
  matrix products: 17.1 us -> 0 us
  between operations: 14.5 us -> 0.73 us
  starting transfers between devices: 12.1 us -> 0 us
    psum x2 -> x0, waiting for transfers between devices: 100 us -> none  [body(): gradient = lax.psum(grad_source + returned, 'edge')]
    ppermute x4 -> x0, waiting for transfers between devices: 74.6 us -> none  [from_behind(): lax.ppermute(value, axis, [(i, (i + by) % length) for i in range(length)])]
    pallas_call x0 -> x1, Pallas kernels: none -> 41.2 us  [body(): pl.pallas_call(functools.partial(kernel, n_dom), out_shape=(jax.ShapeDtyp...]
    scatter-add x6 -> x0, other arithmetic: 35.3 us -> none  [the longest x2 20.9 us: bucket_gradients(): jax.ops.segment_sum(grad_negatives.reshape(-1, feature_width), negative_r...]
    gather x10 -> x0, local copies, waits for them, and re-layouts: 18.4 us -> none  [the longest x2 10.5 us: per_group(): negatives = jnp.take(partner_block, negative_index, axis=0)]
    dot_general x8 -> x0, matrix products: 17.1 us -> none  [the longest x2 5.89 us: group_terms(): jnp.dot(weights, negatives, preferred_element_type=jnp.float32)]
    ppermute x4 -> x0, starting transfers between devices: 12 us -> none  [from_behind(): lax.ppermute(value, axis, [(i, (i + by) % length) for i in range(length)])]
    reduce_sum x6 -> x0, other arithmetic: 5.63 us -> none  [the longest x2 2.64 us: adagrad_step(): new_state = state + jnp.mean(gradient * gradient, axis=1)]
  transfers between devices with their start and end apart: 6 -> 0, of which waited for: 6 -> 0; matrix products, arithmetic and copies ran while one was open for 4% -> 0% of each run, Pallas kernels for 0% -> 0%
where the time goes in v1:
time: 46.4 us; the launch traced here: 46.3 us
  Pallas kernels  41.2 us (89%)
  local copies, waits for them, and re-layouts  4.31 us (9%)
  between operations  0.73 us (2%)
    pallas_call x1, Pallas kernels, body(): pl.pallas_call(functools.partial(kernel, n_dom), out_shape=(jax.ShapeDtyp...  41.2 us
    unnamed x13, local copies, waits for them, and re-layouts  3.14 us
    pallas_call x1, local copies, waits for them, and re-layouts, body(): pl.pallas_call(functools.partial(kernel, n_dom), out_shape=(jax.ShapeDtyp...  1.17 us

profile of v1, /device:TPU:33, one launch (start us, length us, event | category | flops | bytes accessed | tf_op | source)
XLA Modules:
  0.0 46.3 jit_solution(10527676666595129039)
XLA Ops:
  0.6 1.1 %copy.10.rel = bf16[128,800]{1,0:T(8,128)(2,1)S(1)} copy(bf16[128,800]{0,1:T(8,128)(2,1)} %param.9) | data formatting | bytes 409600 | tf_op args[2]
  1.7 0.0 copy-start
  1.7 0.0 copy-start.1
  1.7 0.0 copy-start.2
  1.8 0.0 copy-start.3
  1.8 0.0 copy-start.4
  1.8 1.5 %copy.9.emb = f32[256,800]{1,0:T(8,128)S(1)} copy(f32[256,800]{0,1:T(8,128)} %param.7) | data formatting | bytes 1638400 | tf_op args[0]
  3.2 0.0 copy-done
  3.3 0.0 copy-done.1
  3.3 0.0 copy-done.2
  3.3 0.0 copy-done.3
  3.3 0.0 copy-done.4
  3.3 41.2 %shard_map.86 = (f32[256,800]{1,0:T(8,128)S(1)}, f32[256]{0:T(256)S(1)}) custom-call(f32[256,800]{1,0:T(8,128)S(1)} %copy.9.emb, f32[256]{0:T(256)S(1)} %copy-done.4, bf16[128,800]{1,0:T(8,128)(2,1)S(1)} %copy.10.rel, s32[2,1,256]{2,1,0:T(1,128)S(1)} %copy-done.1, s32[2,1,256]{2,1,0:T(1,128)S(1)} %copy-done.2, s32[2,1,256]{2,1,0:T(1,128)S(1)} %copy-done.3, ...), custom_call_target="tpu_custom_call" | custom-call | tf_op jit(solution)/shard_map/pallas_call | solution.py:307
  44.5 1.2 %copy.11 = f32[256,800]{0,1:T(8,128)} copy(f32[256,800]{1,0:T(8,128)S(1)} %get-tuple-element.2) | data formatting | bytes 1638400 | tf_op jit(solution)/shard_map/pallas_call | solution.py:307
  45.7 0.6 %copy.13 = f32[256]{0:T(256)} copy(f32[256]{0:T(256)S(1)} %get-tuple-element.7) | data formatting | bytes 2048
Async XLA Ops:
  1.7 1.5 %copy-start = (s32[2,1,1,1024]{3,2,1,0:T(1,128)S(1)}, s32[2,1,1,1024]{3,2,1,0:T(1,128)}, u32[]{:S(2)}) copy-start(s32[2,1,1,1024]{3,2,1,0:T(1,128)} %neg.1) | copy-start | bytes 24580
  1.7 1.5 %copy-start.1 = (s32[2,1,256]{2,1,0:T(1,128)S(1)}, s32[2,1,256]{2,1,0:T(1,128)}, u32[]{:S(2)}) copy-start(s32[2,1,256]{2,1,0:T(1,128)} %src.1) | copy-start | bytes 6148
  1.7 1.5 %copy-start.2 = (s32[2,1,256]{2,1,0:T(1,128)S(1)}, s32[2,1,256]{2,1,0:T(1,128)}, u32[]{:S(2)}) copy-start(s32[2,1,256]{2,1,0:T(1,128)} %tgt.1) | copy-start | bytes 6148
  1.8 1.5 %copy-start.3 = (s32[2,1,256]{2,1,0:T(1,128)S(1)}, s32[2,1,256]{2,1,0:T(1,128)}, u32[]{:S(2)}) copy-start(s32[2,1,256]{2,1,0:T(1,128)} %rid.1) | copy-start | bytes 6148
  1.8 1.5 %copy-start.4 = (f32[256]{0:T(256)S(1)}, f32[256]{0:T(256)}, u32[]{:S(2)}) copy-start(f32[256]{0:T(256)} %state.1) | copy-start | bytes 3076

commit v2 on v1

v2 whole, which is shorter than its diff:
```python
import functools

import jax
import jax.numpy as jnp
from jax import lax
from jax.experimental import pallas as pl
from jax.experimental.pallas import tpu as pltpu
from jax.sharding import PartitionSpec as P

MESH = pl.DeviceIdType.MESH
F32 = jnp.float32
BF16 = jnp.bfloat16

learning_rate = 0.1
ROWS = 256
HALF = 128
GROUPS = 4
E = 256
COLS = 800

CHUNKS = ((0, 208, 0), (416, 192, 208))
NATURAL = [(a, n, c) for a, n, c in CHUNKS] + [(a + n, n, c + 400) for a, n, c in CHUNKS]


def chunk(ch):
    a, n, _ = CHUNKS[ch]
    return pl.ds(a, 2 * n)


def parts(ch):
    a, n, _ = CHUNKS[ch]
    return pl.ds(a, n), pl.ds(a + n, n)


def dot(a, b, ca, cb):
    return lax.dot_general(a, b, (((ca,), (cb,)), ((), ())), preferred_element_type=F32)


def kernel(
    n_dom,
    emb, state, rel, src, tgt, rid, neg,
    out_w, out_s,
    w, statev, relv, srcv, tgtv, ridv, negv,
    pack, idx, buf, bt0, bt1, r, q, part, ots, lc, gt, gs, xs, xr,
    load_sem, emb_sem, rel_sem, row_send, row_recv, idx_send, idx_recv, x_send, x_recv,
):
    d = lax.axis_index("dom")
    e = lax.axis_index("edge")
    core = lax.rem(e, 2)
    plane = e - core
    sibling = plane + (1 - core)
    up = [lax.rem(d + k + 1, n_dom) for k in range(2)]
    down = [lax.rem(d + n_dom - k - 1, n_dom) for k in range(2)]
    mine = pl.ds(pl.multiple_of(core * HALF, HALF), HALF)
    other = pl.ds(pl.multiple_of((1 - core) * HALF, HALF), HALF)
    bt = (bt0, bt1)

    index_loads = [
        pltpu.make_async_copy(a, b, load_sem.at[i])
        for i, (a, b) in enumerate(((src, srcv), (tgt, tgtv), (rid, ridv), (neg, negv), (state, statev)))
    ]
    emb_loads = [
        pltpu.make_async_copy(emb.at[pl.ds(c, n), half], w.at[pl.ds(a, n), half], emb_sem.at[j, i])
        for j, half in enumerate((mine, other))
        for i, (a, n, c) in enumerate(NATURAL)
    ]
    rel_loads = [
        pltpu.make_async_copy(rel.at[pl.ds(c, n)], relv.at[pl.ds(a, n)], rel_sem.at[i])
        for i, (a, n, c) in enumerate(NATURAL)
    ]
    for c in index_loads[:4] + emb_loads[:4]:
        c.start()

    barrier = pltpu.get_barrier_semaphore()

    def tell(dom, edge):
        pl.semaphore_signal(barrier, inc=1, device_id=(dom, edge), device_id_type=MESH)

    @pl.when(core == 0)
    def _():
        for k in range(2):
            tell(down[k], plane)
            tell(down[k], plane + 1)
        tell(d, sibling)
        tell(d, 2 - plane)
        tell(d, 3 - plane)

    @pl.when(core == 1)
    def _():
        for k in range(2):
            for g in range(GROUPS):
                tell(up[k], g)
        tell(d, sibling)

    for c in emb_loads[4:] + rel_loads + index_loads[4:]:
        c.start()
    for c in index_loads[:4]:
        c.wait()
    for k in range(2):
        pack[k, 0:1, :] = srcv[k]
        pack[k, 1:2, :] = tgtv[k]
        pack[k, 2:3, :] = ridv[k]
        for j in range(4):
            pack[k, 3 + j : 4 + j, :] = negv[k, 0, :, 256 * j : 256 * (j + 1)]

    pl.semaphore_wait(barrier, 8)

    def idx_copy(k, j, group, dom, edge):
        return pltpu.make_async_remote_copy(
            src_ref=pack.at[k],
            dst_ref=idx.at[k, group],
            send_sem=idx_send.at[k, j],
            recv_sem=idx_recv.at[k, group],
            device_id=(dom, edge),
            device_id_type=MESH,
        )

    def idx_sends(k, act):
        for h in range(2):
            pl.when(e != 2 * h)(lambda h=h: act(idx_copy(k, h, e, d, 2 * h)))
            act(idx_copy(k, 2 + h, e, down[k], 2 * h + 1))

    def idx_waits(k):
        for g in range(GROUPS):
            pl.when(e != g + 4 * core)(lambda g=g: idx_copy(k, 0, g, d, sibling).wait_recv())

    def row_copy(k, way, ch):
        return pltpu.make_async_remote_copy(
            src_ref=buf.at[k, core, chunk(ch), mine],
            dst_ref=buf.at[k, 1 - way, chunk(ch), mine],
            send_sem=row_send.at[k, way, ch],
            recv_sem=row_recv.at[k, core, ch],
            device_id=((up[k], plane), (down[k], plane + 1))[way],
            device_id_type=MESH,
        )

    def row_arrival(k, half, ch):
        lane = pl.ds(half * HALF, HALF)
        return pltpu.make_async_remote_copy(
            src_ref=buf.at[k, core, chunk(ch), lane],
            dst_ref=buf.at[k, 1 - core, chunk(ch), lane],
            send_sem=row_send.at[k, half, ch],
            recv_sem=row_recv.at[k, half, ch],
            device_id=(d, sibling),
            device_id_type=MESH,
        )

    def x_copy(k, ch):
        return pltpu.make_async_remote_copy(
            src_ref=xs.at[k, chunk(ch)],
            dst_ref=xr.at[k, chunk(ch)],
            send_sem=x_send.at[k, ch],
            recv_sem=x_recv.at[k, ch],
            device_id=(d, sibling),
            device_id_type=MESH,
        )

    idx_sends(0, lambda c: c.start())
    for ch in range(2):
        emb_loads[ch].wait()
        emb_loads[2 + ch].wait()
        buf[0, core, chunk(ch), mine] = w[chunk(ch), mine].astype(BF16)
        for way in range(2):
            row_copy(0, way, ch).start()
    idx_sends(1, lambda c: c.start())

    @pl.when(core == 0)
    def _():
        for k in range(2):
            idx[k, e] = pack[k]

    for c in emb_loads[4:]:
        c.wait()
    buf[0, core, :, other] = w[:, other].astype(BF16)
    for c in rel_loads + index_loads[4:]:
        c.wait()

    def prepare(k):
        idx_waits(k)
        at = lax.broadcasted_iota(jnp.int32, (ROWS, E), 0)
        for g in range(GROUPS):
            cols = slice(g * E, (g + 1) * E)
            ots[:, cols] = jnp.where(at == idx[k, g, 0:1, :], 1.0, 0.0).astype(BF16)
            count = jnp.zeros((ROWS, E), F32)
            for j in range(4):
                count += jnp.where(at == idx[k, g, 3 + j : 4 + j, :], 1.0, 0.0)
            lc[:, g : g + 1] = jnp.log(jnp.sum(count, axis=1, keepdims=True))
            kind = jnp.where(at[:HALF] == idx[k, g, 2:3, :], 1.0, 0.0).astype(BF16)
            r[:, cols] = dot(relv[...], kind, 1, 0).astype(BF16)

    def flip(k, ch):
        bt[ch][...] = buf[k, 1, chunk(ch), :].T

    def products(k, ch):
        re, im = parts(ch)
        n = CHUNKS[ch][1]
        for g in range(GROUPS):
            cols = slice(g * E, (g + 1) * E)
            s = dot(buf[k, 0, chunk(ch), :], ots[:, cols], 1, 0)
            rr = r[re, cols].astype(F32)
            ri = r[im, cols].astype(F32)
            q[re, cols] = (s[:n] * rr - s[n:] * ri).astype(BF16)
            q[im, cols] = (s[:n] * ri + s[n:] * rr).astype(BF16)

    def scores():
        for g in range(GROUPS):
            cols = slice(g * E, (g + 1) * E)
            part[:, cols] = dot(bt0[...], q[chunk(0), cols], 1, 0)

    def pulls(k):
        at = lax.broadcasted_iota(jnp.int32, (ROWS, E), 0)
        for g in range(GROUPS):
            cols = slice(g * E, (g + 1) * E)
            score = part[:, cols] + dot(bt1[...], q[chunk(1), cols], 1, 0)
            hit = at == idx[k, g, 1:2, :]
            pos = jnp.sum(jnp.where(hit, score, 0.0), axis=0, keepdims=True)
            z = score + lc[:, g : g + 1]
            top = jnp.maximum(jnp.max(z, axis=0, keepdims=True), pos)
            ez = jnp.exp(z - top)
            ep = jnp.exp(pos - top)
            inv = 1.0 / (jnp.sum(ez, axis=0, keepdims=True) + ep)
            pull = ep * inv - 1.0
            gt[:, cols] = (ez * inv + jnp.where(hit, pull, 0.0)).astype(BF16)

    def source_terms(k, ch):
        re, im = parts(ch)
        n = CHUNKS[ch][1]
        for g in range(GROUPS):
            cols = slice(g * E, (g + 1) * E)
            gq = dot(buf[k, 1, chunk(ch), :], gt[:, cols], 1, 0)
            rr = r[re, cols].astype(F32)
            ri = r[im, cols].astype(F32)
            gs[re, cols] = (gq[:n] * rr + gq[n:] * ri).astype(BF16)
            gs[im, cols] = (gq[n:] * rr - gq[:n] * ri).astype(BF16)

    def update(k, lane):
        g = xs[k, :, lane].astype(F32) + xr[k, :, lane].astype(F32)
        new_s = statev[:, lane] + jnp.sum(g * g, axis=0, keepdims=True) * (1.0 / COLS)
        new_w = w[:, lane] - g * (learning_rate * lax.rsqrt(new_s))
        if k == 0:
            statev[:, lane] = new_s
            w[:, lane] = new_w
            buf[1, core, :, lane] = new_w.astype(BF16)
        else:
            out_s[:, lane] = new_s
            out_w[:, lane] = new_w

    for k in range(2):
        prepare(k)

        @pl.when(core == 0)
        def _():
            for ch in range(2):
                products(k, ch)

        @pl.when(core == 1)
        def _():
            for ch in range(2):
                flip(k, ch)

        for ch in range(2):
            for half in range(2):
                row_arrival(k, half, ch).wait_recv()
            pl.when(core == 0)(lambda: flip(k, ch))
            pl.when(core == 1)(lambda: products(k, ch))
            if ch == 0:
                scores()
        pulls(k)
        for ch in range(2):

            @pl.when(core == 0)
            def _():
                source_terms(k, ch)
                xs[k, chunk(ch)] = dot(gs[chunk(ch), :], ots[...], 1, 1).astype(BF16)

            @pl.when(core == 1)
            def _():
                xs[k, chunk(ch)] = dot(q[chunk(ch), :], gt[...], 1, 1).astype(BF16)

            x_copy(k, ch).start()
        for ch in range(2):
            x_copy(k, ch).wait_recv()
        update(k, mine)
        if k == 0:
            for ch in range(2):
                for way in range(2):
                    row_copy(1, way, ch).start()
        update(k, other)

    for k in range(2):
        idx_sends(k, lambda c: c.wait_send())
        for ch in range(2):
            x_copy(k, ch).wait_send()
            for way in range(2):
                row_copy(k, way, ch).wait_send()


def write_out(w, s, out_w, out_s, sem):
    copies = [
        pltpu.make_async_copy(w.at[pl.ds(a, n)], out_w.at[pl.ds(c, n)], sem.at[i])
        for i, (a, n, c) in enumerate(NATURAL)
    ]
    copies.append(pltpu.make_async_copy(s, out_s, sem.at[4]))
    for c in copies:
        c.start()
    for c in copies:
        c.wait()


def solution(mesh):
    n_dom = mesh.shape["dom"]

    def body(embedding, adagrad_state, relation_table, source_row, target_row, relation_id, negative_row):
        vmem = pl.BlockSpec(memory_space=pltpu.VMEM)
        hbm = pl.BlockSpec(memory_space=pltpu.HBM)
        dma = pltpu.SemaphoreType.DMA
        new_w, new_s = pl.pallas_call(
            functools.partial(kernel, n_dom),
            out_shape=(pltpu.VMEM((COLS, ROWS), F32), pltpu.VMEM((1, ROWS), F32)),
            in_specs=[hbm] * 7,
            out_specs=(vmem, vmem),
            scratch_shapes=[
                pltpu.VMEM((COLS, ROWS), F32),
                pltpu.VMEM((1, ROWS), F32),
                pltpu.VMEM((COLS, 128), BF16),
                pltpu.VMEM(source_row.shape, jnp.int32),
                pltpu.VMEM(target_row.shape, jnp.int32),
                pltpu.VMEM(relation_id.shape, jnp.int32),
                pltpu.VMEM(negative_row.shape, jnp.int32),
                pltpu.VMEM((2, 8, E), jnp.int32),
                pltpu.VMEM((2, GROUPS, 8, E), jnp.int32),
                pltpu.VMEM((2, 2, COLS, ROWS), BF16),
                pltpu.VMEM((ROWS, 2 * CHUNKS[0][1]), BF16),
                pltpu.VMEM((ROWS, 2 * CHUNKS[1][1]), BF16),
                pltpu.VMEM((COLS, GROUPS * E), BF16),
                pltpu.VMEM((COLS, GROUPS * E), BF16),
                pltpu.VMEM((ROWS, GROUPS * E), F32),
                pltpu.VMEM((ROWS, GROUPS * E), BF16),
                pltpu.VMEM((ROWS, GROUPS), F32),
                pltpu.VMEM((ROWS, GROUPS * E), BF16),
                pltpu.VMEM((COLS, GROUPS * E), BF16),
                pltpu.VMEM((2, COLS, ROWS), BF16),
                pltpu.VMEM((2, COLS, ROWS), BF16),
                dma((5,)),
                dma((2, 4)),
                dma((4,)),
                dma((2, 2, 2)),
                dma((2, 2, 2)),
                dma((2, 4)),
                dma((2, 4)),
                dma((2, 2)),
                dma((2, 2)),
            ],
            compiler_params=pltpu.CompilerParams(
                collective_id=0, has_side_effects=True, vmem_limit_bytes=32 * 2**20
            ),
        )(
            *(
                pltpu.with_memory_space_constraint(x, pltpu.HBM)
                for x in (
                    embedding.T,
                    adagrad_state.reshape(1, ROWS),
                    relation_table.T,
                    source_row,
                    target_row,
                    relation_id,
                    negative_row,
                )
            )
        )
        new_w, new_s = pl.pallas_call(
            write_out,
            out_shape=(pltpu.HBM((COLS, ROWS), F32), pltpu.HBM((1, ROWS), F32)),
            in_specs=[vmem, vmem],
            out_specs=(hbm, hbm),
            scratch_shapes=[dma((5,))],
        )(*(pltpu.with_memory_space_constraint(x, pltpu.VMEM) for x in (new_w, new_s)))
        return new_w.T, new_s.reshape(ROWS)

    in_specs = (
        P("dom", None),
        P("dom"),
        P(),
        P(None, "dom", "edge"),
        P(None, "dom", "edge"),
        P(None, "dom", "edge"),
        P(None, "dom", "edge", None),
    )
    out_specs = (P("dom", None), P("dom"))
    return jax.shard_map(body, mesh=mesh, in_specs=in_specs, out_specs=out_specs, check_vma=False)
```

time: 46.4 us -> 39.7 us (0.86)
  local copies, waits for them, and re-layouts: 4.31 us -> 0 us
  Pallas kernels: 41.2 us -> 38.9 us
    unnamed x13 -> x0, local copies, waits for them, and re-layouts: 3.14 us -> none
    pallas_call x1 -> x2, Pallas kernels: 41.2 us -> 38.9 us  [the longest x1 38 us: body(): pl.pallas_call(functools.partial(kernel, n_dom), out_shape=(pltpu.VMEM((C...]
    pallas_call x1 -> x0, local copies, waits for them, and re-layouts: 1.17 us -> none  [body(): pl.pallas_call(functools.partial(kernel, n_dom), out_shape=(jax.ShapeDtyp...]
where the time goes in v2:
time: 39.7 us; the launch traced here: 39.6 us
  Pallas kernels  38.9 us (98%)
  between operations  0.64 us (2%)
    pallas_call x1, Pallas kernels, body(): pl.pallas_call(functools.partial(kernel, n_dom), out_shape=(pltpu.VMEM((C...  38 us
    pallas_call x1, Pallas kernels, body(): pl.pallas_call(write_out, out_shape=(pltpu.HBM((COLS, ROWS), F32), pltpu....  0.93 us

profile of v2, /device:TPU:33, one launch (start us, length us, event | category | flops | bytes accessed | tf_op | source)
XLA Modules:
  0.0 39.6 jit_solution(7619346419104682748)
XLA Ops:
  0.6 38.0 %shard_map.86 = (f32[800,256]{1,0:T(8,128)S(1)}, f32[1,256]{1,0:T(1,128)S(1)}) custom-call(f32[800,256]{1,0:T(8,128)} %bitcast.5, f32[1,256]{1,0:T(1,128)} %bitcast.7, bf16[800,128]{1,0:T(8,128)(2,1)} %bitcast.6, s32[2,1,256]{2,1,0:T(1,128)} %src.1, s32[2,1,256]{2,1,0:T(1,128)} %tgt.1, s32[2,1,256]{2,1,0:T(1,128)} %rid.1, s32[2,1,1,1024]{3,2,1,0:T(1,128)} %neg.1), custom_call_target="tpu_custom_call" | custom-call | tf_op jit(solution)/shard_map/pallas_call | solution.py:317
  38.6 0.9 %shard_map.87 = (f32[800,256]{1,0:T(8,128)}, f32[1,256]{1,0:T(1,128)}) custom-call(f32[800,256]{1,0:T(8,128)S(1)} %get-tuple-element.6.w, f32[1,256]{1,0:T(1,128)S(1)} %get-tuple-element.7.s), custom_call_target="tpu_custom_call" | custom-call | tf_op jit(solution)/shard_map/pallas_call | solution.py:371

commit v3 on v2

v3 whole, which is shorter than its diff:
```python
import functools

import jax
import jax.numpy as jnp
from jax import lax
from jax.experimental import pallas as pl
from jax.experimental.pallas import tpu as pltpu
from jax.sharding import PartitionSpec as P

MESH = pl.DeviceIdType.MESH
F32 = jnp.float32
BF16 = jnp.bfloat16

learning_rate = 0.1
ROWS = 256
HALF = 128
GROUPS = 4
E = 256
COLS = 800

CHUNKS = ((0, 128, 0), (256, 128, 128), (512, 144, 256))
N_CH = len(CHUNKS)
ACROSS = 0
SPANS = ((0, 2), (2, 3))
NATURAL = [(a, n, c) for a, n, c in CHUNKS] + [(a + n, n, c + 400) for a, n, c in CHUNKS]


def chunk(ch):
    a, n, _ = CHUNKS[ch]
    return pl.ds(a, 2 * n)


def parts(ch):
    a, n, _ = CHUNKS[ch]
    return pl.ds(a, n), pl.ds(a + n, n)


def span(j):
    first, last = CHUNKS[SPANS[j][0]], CHUNKS[SPANS[j][1] - 1]
    return pl.ds(first[0], last[0] + 2 * last[1] - first[0])


def dot(a, b, ca, cb):
    return lax.dot_general(a, b, (((ca,), (cb,)), ((), ())), preferred_element_type=F32)


def kernel(
    n_dom,
    emb, state, rel, src, tgt, rid, neg,
    out_w, out_s,
    w, statev, relv, srcv, tgtv, ridv, negv,
    pack, sib_pack, idx, buf, bt, r, q, part, ots, lc, gt, gs, xs, xr,
    load_sem, emb_sem, rel_sem, row_send, row_recv, idx_send, idx_recv, x_send, x_recv, relay,
):
    d = lax.axis_index("dom")
    e = lax.axis_index("edge")
    core = lax.rem(e, 2)
    plane = e - core
    sibling = plane + (1 - core)
    up = [lax.rem(d + k + 1, n_dom) for k in range(2)]
    down = [lax.rem(d + n_dom - k - 1, n_dom) for k in range(2)]
    mine = pl.ds(pl.multiple_of(core * HALF, HALF), HALF)
    other = pl.ds(pl.multiple_of((1 - core) * HALF, HALF), HALF)

    index_loads = [
        pltpu.make_async_copy(a, b, load_sem.at[i])
        for i, (a, b) in enumerate(((src, srcv), (tgt, tgtv), (rid, ridv), (neg, negv), (state, statev)))
    ]
    emb_loads = [
        pltpu.make_async_copy(emb.at[pl.ds(c, n), half], w.at[pl.ds(a, n), half], emb_sem.at[j, i])
        for j, half in enumerate((mine, other))
        for i, (a, n, c) in enumerate(NATURAL)
    ]
    rel_loads = [
        pltpu.make_async_copy(rel.at[pl.ds(c, n)], relv.at[pl.ds(a, n)], rel_sem.at[i])
        for i, (a, n, c) in enumerate(NATURAL)
    ]
    for c in index_loads[:4] + emb_loads[: 2 * N_CH]:
        c.start()

    barrier = pltpu.get_barrier_semaphore()

    def tell(dom, edge):
        pl.semaphore_signal(barrier, inc=1, device_id=(dom, edge), device_id_type=MESH)

    @pl.when(core == 0)
    def _():
        tell(down[0], plane)
        tell(d, 3 - plane)

    @pl.when(core == 1)
    def _():
        tell(d, plane)
        tell(up[0], plane)
        tell(up[0], 3 - plane)

    for c in index_loads[:4]:
        c.wait()
    for k in range(2):
        pack[k, 0:1, :] = srcv[k]
        pack[k, 1:2, :] = tgtv[k]
        pack[k, 2:3, :] = ridv[k]
        for j in range(4):
            pack[k, 3 + j : 4 + j, :] = negv[k, 0, :, 256 * j : 256 * (j + 1)]

    order = [lax.rem(plane + o, GROUPS) for o in range(GROUPS)]

    def pass_on(j, dom, edge):
        pl.semaphore_signal(relay.at[j], inc=1, device_id=(dom, edge), device_id_type=MESH)

    @pl.when(core == 0)
    def _():
        pl.semaphore_wait(barrier, 3)
        pass_on(2, d, sibling)
        pass_on(0, up[0], plane)
        pass_on(0, down[0], plane + 1)

    @pl.when(core == 1)
    def _():
        pl.semaphore_wait(relay.at[2], 1)

    def idx_copy(j, source, target, recv, dom, edge):
        return pltpu.make_async_remote_copy(
            src_ref=source,
            dst_ref=target,
            send_sem=idx_send.at[j],
            recv_sem=idx_recv.at[recv],
            device_id=(dom, edge),
            device_id_type=MESH,
        )

    to_sibling = idx_copy(0, pack, sib_pack, 5, d, sibling)
    to_own = idx_copy(0, pack, idx.at[:, e], e, d, plane)
    to_down = idx_copy(1, pack.at[0], idx.at[0, e], e, down[0], plane + 1)
    to_down2 = idx_copy(2, idx.at[1], idx.at[1], 4, down[1], plane + 1)
    across = [
        idx_copy(2, pack, idx.at[:, e], e, d, 2 - plane),
        idx_copy(3, sib_pack, idx.at[:, e - core], e - core, d, 2 - plane),
        idx_copy(4, pack.at[0], idx.at[0, e], e, down[0], 3 - plane),
        idx_copy(5, sib_pack.at[0], idx.at[0, e - core], e - core, down[0], 3 - plane),
    ]

    def idx_wait(k, g):
        @pl.when(core == 0)
        def _():
            if k == 0:
                pl.when(e != g)(lambda: idx_copy(0, pack, idx.at[:, g], g, d, sibling).wait_recv())

        @pl.when(core == 1)
        def _():
            if k == 0:
                idx_copy(1, pack.at[0], idx.at[0, g], g, d, sibling).wait_recv()
            else:
                pl.when(g == order[0])(to_down2.wait_recv)

    def row_copy(k, way, ch):
        return pltpu.make_async_remote_copy(
            src_ref=buf.at[k, core, core, chunk(ch)],
            dst_ref=buf.at[k, 1 - way, core, chunk(ch)],
            send_sem=row_send.at[k, way, ch],
            recv_sem=row_recv.at[k, core, ch],
            device_id=((up[k], plane), (down[k], plane + 1))[way],
            device_id_type=MESH,
        )

    def row_arrival(k, half, ch):
        return pltpu.make_async_remote_copy(
            src_ref=buf.at[k, core, half, chunk(ch)],
            dst_ref=buf.at[k, 1 - core, half, chunk(ch)],
            send_sem=row_send.at[k, half, ch],
            recv_sem=row_recv.at[k, half, ch],
            device_id=(d, sibling),
            device_id_type=MESH,
        )

    def x_copy(k, j):
        return pltpu.make_async_remote_copy(
            src_ref=xs.at[k, span(j)],
            dst_ref=xr.at[k, span(j)],
            send_sem=x_send.at[k, j],
            recv_sem=x_recv.at[k, j],
            device_id=(d, sibling),
            device_id_type=MESH,
        )

    pl.when(core == 0)(to_sibling.start)
    pl.when(core == 1)(to_own.start)
    to_down.start()
    for ch in range(N_CH):
        emb_loads[ch].wait()
        emb_loads[N_CH + ch].wait()
        buf[0, core, core, chunk(ch)] = w[chunk(ch), mine].astype(BF16)
        for way in range(2):
            row_copy(0, way, ch).start()
        if ch == ACROSS:

            @pl.when(core == 1)
            def _():
                to_sibling.wait_recv()
                pl.semaphore_wait(barrier, 2)
                for c in across:
                    c.start()

    for c in emb_loads[2 * N_CH :] + rel_loads + index_loads[4:]:
        c.start()

    @pl.when(core == 0)
    def _():
        for k in range(2):
            idx[k, e] = pack[k]

    for c in emb_loads[2 * N_CH :]:
        c.wait()
    buf[0, core, 1 - core] = w[:, other].astype(BF16)
    for c in rel_loads + index_loads[4:]:
        c.wait()

    def prepare(k, g):
        idx_wait(k, g)
        cols = pl.ds(pl.multiple_of(g * E, E), E)
        at = lax.broadcasted_iota(jnp.int32, (ROWS, E), 0)
        ots[:, cols] = jnp.where(at == idx[k, g, 0:1, :], 1.0, 0.0).astype(BF16)
        count = jnp.zeros((ROWS, E), F32)
        for j in range(4):
            count += jnp.where(at == idx[k, g, 3 + j : 4 + j, :], 1.0, 0.0)
        lc[g] = jnp.log(jnp.sum(count, axis=1, keepdims=True))
        kind = jnp.where(at[:HALF] == idx[k, g, 2:3, :], 1.0, 0.0).astype(BF16)
        r[:, cols] = dot(relv[...], kind, 1, 0).astype(BF16)

    def whole(k, slot, ch):
        return jnp.concatenate([buf[k, slot, half, chunk(ch)] for half in range(2)], axis=1)

    def flip(k, ch):
        for half in range(2):
            bt[half * HALF : (half + 1) * HALF, chunk(ch)] = buf[k, 1, half, chunk(ch)].T

    def products(k, ch, g):
        re, im = parts(ch)
        n = CHUNKS[ch][1]
        cols = pl.ds(pl.multiple_of(g * E, E), E)
        s = dot(whole(k, 0, ch), ots[:, cols], 1, 0)
        rr = r[re, cols].astype(F32)
        ri = r[im, cols].astype(F32)
        q[re, cols] = (s[:n] * rr - s[n:] * ri).astype(BF16)
        q[im, cols] = (s[:n] * ri + s[n:] * rr).astype(BF16)

    def scores(ch):
        for g in range(GROUPS):
            cols = slice(g * E, (g + 1) * E)
            new = dot(bt[:, chunk(ch)], q[chunk(ch), cols], 1, 0)
            part[:, cols] = new if ch == 0 else part[:, cols] + new

    def pulls(k):
        at = lax.broadcasted_iota(jnp.int32, (ROWS, E), 0)
        for g in range(GROUPS):
            cols = slice(g * E, (g + 1) * E)
            score = part[:, cols] + dot(bt[:, chunk(N_CH - 1)], q[chunk(N_CH - 1), cols], 1, 0)
            hit = at == idx[k, g, 1:2, :]
            pos = jnp.sum(jnp.where(hit, score, 0.0), axis=0, keepdims=True)
            z = score + lc[g]
            top = jnp.maximum(jnp.max(z, axis=0, keepdims=True), pos)
            ez = jnp.exp(z - top)
            ep = jnp.exp(pos - top)
            inv = 1.0 / (jnp.sum(ez, axis=0, keepdims=True) + ep)
            pull = ep * inv - 1.0
            gt[:, cols] = (ez * inv + jnp.where(hit, pull, 0.0)).astype(BF16)

    def source_terms(k, ch):
        re, im = parts(ch)
        n = CHUNKS[ch][1]
        for g in range(GROUPS):
            cols = slice(g * E, (g + 1) * E)
            gq = dot(whole(k, 1, ch), gt[:, cols], 1, 0).astype(BF16)
            rr, ri = r[re, cols], r[im, cols]
            gs[re, cols] = gq[:n] * rr + gq[n:] * ri
            gs[im, cols] = gq[n:] * rr - gq[:n] * ri

    def update(k, half, lane):
        g = xs[k, :, lane].astype(F32) + xr[k, :, lane].astype(F32)
        new_s = statev[:, lane] + jnp.sum(g * g, axis=0, keepdims=True) * (1.0 / COLS)
        new_w = w[:, lane] - g * (learning_rate * lax.rsqrt(new_s))
        if k == 0:
            statev[:, lane] = new_s
            w[:, lane] = new_w
            buf[1, core, half] = new_w.astype(BF16)
        else:
            out_s[:, lane] = new_s
            out_w[:, lane] = new_w

    for k in range(2):
        for o in range(GROUPS):
            prepare(k, order[o])

            @pl.when(core == 0)
            def _():
                for ch in range(N_CH):
                    products(k, ch, order[o])

        @pl.when(core == 1)
        def _():
            for ch in range(N_CH):
                flip(k, ch)

        for ch in range(N_CH):
            for half in range(2):
                row_arrival(k, half, ch).wait_recv()
            pl.when(core == 0)(lambda: flip(k, ch))

            @pl.when(core == 1)
            def _():
                for g in range(GROUPS):
                    products(k, ch, g)

            if ch < N_CH - 1:
                scores(ch)
        pulls(k)
        for j in range(2):

            @pl.when(core == 0)
            def _():
                for ch in range(*SPANS[j]):
                    source_terms(k, ch)
                xs[k, span(j)] = dot(gs[span(j), :], ots[...], 1, 1).astype(BF16)

            @pl.when(core == 1)
            def _():
                xs[k, span(j)] = dot(q[span(j), :], gt[...], 1, 1).astype(BF16)

            x_copy(k, j).start()
        if k == 0:
            pl.semaphore_wait(relay.at[0], 1)
            pass_on(1, d, sibling)
        for j in range(2):
            x_copy(k, j).wait_recv()
        update(k, core, mine)
        if k == 0:
            pl.semaphore_wait(relay.at[1], 1)
            pl.when(core == 0)(to_down2.start)
            for ch in range(N_CH):
                for way in range(2):
                    row_copy(1, way, ch).start()
        update(k, 1 - core, other)

    to_down.wait_send()

    @pl.when(core == 0)
    def _():
        to_sibling.wait_send()
        to_down2.wait_send()

    @pl.when(core == 1)
    def _():
        for c in [to_own] + across:
            c.wait_send()

    for k in range(2):
        for j in range(2):
            x_copy(k, j).wait_send()
        for ch in range(N_CH):
            for way in range(2):
                row_copy(k, way, ch).wait_send()


def write_out(w, s, out_w, out_s, sem):
    copies = [
        pltpu.make_async_copy(w.at[pl.ds(a, n)], out_w.at[pl.ds(c, n)], sem.at[i])
        for i, (a, n, c) in enumerate(NATURAL)
    ]
    copies.append(pltpu.make_async_copy(s, out_s, sem.at[2 * N_CH]))
    for c in copies:
        c.start()
    for c in copies:
        c.wait()


def solution(mesh):
    n_dom = mesh.shape["dom"]

    def body(embedding, adagrad_state, relation_table, source_row, target_row, relation_id, negative_row):
        vmem = pl.BlockSpec(memory_space=pltpu.VMEM)
        hbm = pl.BlockSpec(memory_space=pltpu.HBM)
        dma = pltpu.SemaphoreType.DMA
        new_w, new_s = pl.pallas_call(
            functools.partial(kernel, n_dom),
            out_shape=(pltpu.VMEM((COLS, ROWS), F32), pltpu.VMEM((1, ROWS), F32)),
            in_specs=[hbm] * 7,
            out_specs=(vmem, vmem),
            scratch_shapes=[
                pltpu.VMEM((COLS, ROWS), F32),
                pltpu.VMEM((1, ROWS), F32),
                pltpu.VMEM((COLS, 128), BF16),
                pltpu.VMEM(source_row.shape, jnp.int32),
                pltpu.VMEM(target_row.shape, jnp.int32),
                pltpu.VMEM(relation_id.shape, jnp.int32),
                pltpu.VMEM(negative_row.shape, jnp.int32),
                pltpu.VMEM((2, 8, E), jnp.int32),
                pltpu.VMEM((2, 8, E), jnp.int32),
                pltpu.VMEM((2, GROUPS, 8, E), jnp.int32),
                pltpu.VMEM((2, 2, 2, COLS, HALF), BF16),
                pltpu.VMEM((ROWS, COLS), BF16),
                pltpu.VMEM((COLS, GROUPS * E), BF16),
                pltpu.VMEM((COLS, GROUPS * E), BF16),
                pltpu.VMEM((ROWS, GROUPS * E), F32),
                pltpu.VMEM((ROWS, GROUPS * E), BF16),
                pltpu.VMEM((GROUPS, ROWS, 1), F32),
                pltpu.VMEM((ROWS, GROUPS * E), BF16),
                pltpu.VMEM((COLS, GROUPS * E), BF16),
                pltpu.VMEM((2, COLS, ROWS), BF16),
                pltpu.VMEM((2, COLS, ROWS), BF16),
                dma((5,)),
                dma((2, 2 * N_CH)),
                dma((2 * N_CH,)),
                dma((2, 2, N_CH)),
                dma((2, 2, N_CH)),
                dma((6,)),
                dma((6,)),
                dma((2, 2)),
                dma((2, 2)),
                pltpu.SemaphoreType.REGULAR((3,)),
            ],
            compiler_params=pltpu.CompilerParams(
                collective_id=0, has_side_effects=True, vmem_limit_bytes=32 * 2**20
            ),
        )(
            *(
                pltpu.with_memory_space_constraint(x, pltpu.HBM)
                for x in (
                    embedding.T,
                    adagrad_state.reshape(1, ROWS),
                    relation_table.T,
                    source_row,
                    target_row,
                    relation_id,
                    negative_row,
                )
            )
        )
        new_w, new_s = pl.pallas_call(
            write_out,
            out_shape=(pltpu.HBM((COLS, ROWS), F32), pltpu.HBM((1, ROWS), F32)),
            in_specs=[vmem, vmem],
            out_specs=(hbm, hbm),
            scratch_shapes=[dma((2 * N_CH + 1,))],
        )(*(pltpu.with_memory_space_constraint(x, pltpu.VMEM) for x in (new_w, new_s)))
        return new_w.T, new_s.reshape(ROWS)

    in_specs = (
        P("dom", None),
        P("dom"),
        P(),
        P(None, "dom", "edge"),
        P(None, "dom", "edge"),
        P(None, "dom", "edge"),
        P(None, "dom", "edge", None),
    )
    out_specs = (P("dom", None), P("dom"))
    return jax.shard_map(body, mesh=mesh, in_specs=in_specs, out_specs=out_specs, check_vma=False)
```

time: 39.7 us -> 39.1 us (0.985)
  Pallas kernels: 38.9 us -> 38.1 us
    pallas_call x1, Pallas kernels: 38 us -> 37.2 us  [body(): pl.pallas_call(functools.partial(kernel, n_dom), out_shape=(pltpu.VMEM((C...]
where the time goes in v3:
time: 39.1 us; the launch traced here: 38.9 us
  Pallas kernels  38.1 us (97%)
  between operations  0.8 us (2%)
    pallas_call x1, Pallas kernels, body(): pl.pallas_call(functools.partial(kernel, n_dom), out_shape=(pltpu.VMEM((C...  37.2 us
    pallas_call x1, Pallas kernels, body(): pl.pallas_call(write_out, out_shape=(pltpu.HBM((COLS, ROWS), F32), pltpu....  0.95 us

profile of v3, /device:TPU:33, one launch (start us, length us, event | category | flops | bytes accessed | tf_op | source)
XLA Modules:
  0.0 38.9 jit_solution(5062164943371636252)
XLA Ops:
  0.6 37.2 %shard_map.86 = (f32[800,256]{1,0:T(8,128)S(1)}, f32[1,256]{1,0:T(1,128)S(1)}) custom-call(f32[800,256]{1,0:T(8,128)} %bitcast.5, f32[1,256]{1,0:T(1,128)} %bitcast.7, bf16[800,128]{1,0:T(8,128)(2,1)} %bitcast.6, s32[2,1,256]{2,1,0:T(1,128)} %src.1, s32[2,1,256]{2,1,0:T(1,128)} %tgt.1, s32[2,1,256]{2,1,0:T(1,128)} %rid.1, s32[2,1,1,1024]{3,2,1,0:T(1,128)} %neg.1), custom_call_target="tpu_custom_call" | custom-call | tf_op jit(solution)/shard_map/pallas_call | solution.py:383
  37.8 0.9 %shard_map.87 = (f32[800,256]{1,0:T(8,128)}, f32[1,256]{1,0:T(1,128)}) custom-call(f32[800,256]{1,0:T(8,128)S(1)} %get-tuple-element.6.w, f32[1,256]{1,0:T(1,128)S(1)} %get-tuple-element.7.s), custom_call_target="tpu_custom_call" | custom-call | tf_op jit(solution)/shard_map/pallas_call | solution.py:438

commit v4 on v3

--- a/solution.py
+++ b/solution.py
@@ -18,9 +18,9 @@
 E = 256
 COLS = 800
 
-CHUNKS = ((0, 128, 0), (256, 128, 128), (512, 144, 256))
+CHUNKS = ((0, 192, 0), (384, 128, 192), (640, 80, 320))
 N_CH = len(CHUNKS)
-ACROSS = 0
+RING = 8
 SPANS = ((0, 2), (2, 3))
 NATURAL = [(a, n, c) for a, n, c in CHUNKS] + [(a + n, n, c + 400) for a, n, c in CHUNKS]
 
@@ -49,7 +49,7 @@
     emb, state, rel, src, tgt, rid, neg,
     out_w, out_s,
     w, statev, relv, srcv, tgtv, ridv, negv,
-    pack, sib_pack, idx, buf, bt, r, q, part, ots, lc, gt, gs, xs, xr,
+    pack, idx, buf, bt, r, q, part, ots, lc, gt, gs, xs, xr,
     load_sem, emb_sem, rel_sem, row_send, row_recv, idx_send, idx_recv, x_send, x_recv, relay,
 ):
     d = lax.axis_index("dom")
@@ -61,6 +61,26 @@
     down = [lax.rem(d + n_dom - k - 1, n_dom) for k in range(2)]
     mine = pl.ds(pl.multiple_of(core * HALF, HALF), HALF)
     other = pl.ds(pl.multiple_of((1 - core) * HALF, HALF), HALF)
+
+    barrier = pltpu.get_barrier_semaphore()
+
+    def tell(dom, edge):
+        pl.semaphore_signal(barrier, inc=1, device_id=(dom, edge), device_id_type=MESH)
+
+    @pl.when(core == 0)
+    def _():
+        tell(down[0], plane)
+        tell(d, sibling)
+        tell(d, 3 - plane)
+
+    first = lax.rem(d, RING) == 0
+    last = lax.rem(d, RING) == RING - 1
+
+    @pl.when(core == 1)
+    def _():
+        tell(up[0], plane)
+        tell(d, plane)
+        pl.when(jnp.logical_not(last))(lambda: tell(up[0], 3 - plane))
 
     index_loads = [
         pltpu.make_async_copy(a, b, load_sem.at[i])
@@ -78,22 +98,6 @@
     for c in index_loads[:4] + emb_loads[: 2 * N_CH]:
         c.start()
 
-    barrier = pltpu.get_barrier_semaphore()
-
-    def tell(dom, edge):
-        pl.semaphore_signal(barrier, inc=1, device_id=(dom, edge), device_id_type=MESH)
-
-    @pl.when(core == 0)
-    def _():
-        tell(down[0], plane)
-        tell(d, 3 - plane)
-
-    @pl.when(core == 1)
-    def _():
-        tell(d, plane)
-        tell(up[0], plane)
-        tell(up[0], 3 - plane)
-
     for c in index_loads[:4]:
         c.wait()
     for k in range(2):
@@ -108,16 +112,10 @@
     def pass_on(j, dom, edge):
         pl.semaphore_signal(relay.at[j], inc=1, device_id=(dom, edge), device_id_type=MESH)
 
-    @pl.when(core == 0)
-    def _():
-        pl.semaphore_wait(barrier, 3)
-        pass_on(2, d, sibling)
-        pass_on(0, up[0], plane)
-        pass_on(0, down[0], plane + 1)
-
-    @pl.when(core == 1)
-    def _():
-        pl.semaphore_wait(relay.at[2], 1)
+    for ch in range(N_CH):
+        emb_loads[ch].wait()
+        emb_loads[N_CH + ch].wait()
+        buf[0, core, core, chunk(ch)] = w[chunk(ch), mine].astype(BF16)
 
     def idx_copy(j, source, target, recv, dom, edge):
         return pltpu.make_async_remote_copy(
@@ -129,29 +127,71 @@
             device_id_type=MESH,
         )
 
-    to_sibling = idx_copy(0, pack, sib_pack, 5, d, sibling)
     to_own = idx_copy(0, pack, idx.at[:, e], e, d, plane)
     to_down = idx_copy(1, pack.at[0], idx.at[0, e], e, down[0], plane + 1)
     to_down2 = idx_copy(2, idx.at[1], idx.at[1], 4, down[1], plane + 1)
-    across = [
-        idx_copy(2, pack, idx.at[:, e], e, d, 2 - plane),
-        idx_copy(3, sib_pack, idx.at[:, e - core], e - core, d, 2 - plane),
-        idx_copy(4, pack.at[0], idx.at[0, e], e, down[0], 3 - plane),
-        idx_copy(5, sib_pack.at[0], idx.at[0, e - core], e - core, down[0], 3 - plane),
-    ]
-
-    def idx_wait(k, g):
+    across = idx_copy(4, pack, idx.at[:, e], e, d, 2 - plane)
+    down_across = idx_copy(3, pack.at[0], idx.at[0, e], e, down[0], 3 - plane)
+    both = pl.ds(2 - plane, 2)
+    onward = idx_copy(0, idx.at[0, both], idx.at[0, both], 2 - plane, down[0], plane + 1)
+
+    def cross(heard):
+        @pl.when(core == 1)
+        def _():
+            pl.semaphore_wait(barrier, heard)
+            pass_on(3, d, sibling)
+
+        pl.when(core == 0)(lambda: pl.semaphore_wait(relay.at[3], 1))
+        across.start()
+
+    @pl.when(first)
+    def _():
+        cross(2)
+        pl.when(core == 1)(to_own.start)
+
+    @pl.when(core == 0)
+    def _():
+        pl.semaphore_wait(barrier, 3)
+        pass_on(2, d, sibling)
+        pass_on(0, up[0], plane)
+        pass_on(0, down[0], plane + 1)
+
+    @pl.when(core == 1)
+    def _():
+        pl.semaphore_wait(relay.at[2], 1)
+
+    def send_onward():
+        for h in (2, 3):
+            idx_copy(0, pack, idx.at[:, order[h]], order[h], d, sibling).wait_recv()
+        onward.start()
+
+    def idx_wait(k, o):
+        g = order[o]
+
         @pl.when(core == 0)
         def _():
-            if k == 0:
+            if k == 0 and o < 2:
                 pl.when(e != g)(lambda: idx_copy(0, pack, idx.at[:, g], g, d, sibling).wait_recv())
+            elif k == 0 and o == 2:
+
+                @pl.when(jnp.logical_not(first))
+                def _():
+                    for h in (2, 3):
+                        idx_copy(0, pack, idx.at[:, order[h]], order[h], d, sibling).wait_recv()
 
         @pl.when(core == 1)
         def _():
-            if k == 0:
+            if k == 0 and o < 2:
                 idx_copy(1, pack.at[0], idx.at[0, g], g, d, sibling).wait_recv()
-            else:
-                pl.when(g == order[0])(to_down2.wait_recv)
+            elif k == 0 and o == 2:
+                pl.when(last)(onward.wait_recv)
+
+                @pl.when(jnp.logical_not(last))
+                def _():
+                    for h in (2, 3):
+                        idx_copy(1, pack.at[0], idx.at[0, order[h]], order[h], d, sibling).wait_recv()
+            elif k == 1 and o == 0:
+                to_down2.wait_recv()
 
     def row_copy(k, way, ch):
         return pltpu.make_async_remote_copy(
@@ -183,23 +223,18 @@
             device_id_type=MESH,
         )
 
-    pl.when(core == 0)(to_sibling.start)
-    pl.when(core == 1)(to_own.start)
+    pl.when(jnp.logical_and(core == 1, jnp.logical_not(first)))(to_own.start)
     to_down.start()
+    pl.when(jnp.logical_and(core == 0, first))(send_onward)
     for ch in range(N_CH):
-        emb_loads[ch].wait()
-        emb_loads[N_CH + ch].wait()
-        buf[0, core, core, chunk(ch)] = w[chunk(ch), mine].astype(BF16)
-        for way in range(2):
+        for way in (1, 0):
             row_copy(0, way, ch).start()
-        if ch == ACROSS:
-
-            @pl.when(core == 1)
+        if ch == 0:
+
+            @pl.when(jnp.logical_not(first))
             def _():
-                to_sibling.wait_recv()
-                pl.semaphore_wait(barrier, 2)
-                for c in across:
-                    c.start()
+                cross(3)
+                down_across.start()
 
     for c in emb_loads[2 * N_CH :] + rel_loads + index_loads[4:]:
         c.start()
@@ -215,8 +250,9 @@
     for c in rel_loads + index_loads[4:]:
         c.wait()
 
-    def prepare(k, g):
-        idx_wait(k, g)
+    def prepare(k, o):
+        idx_wait(k, o)
+        g = order[o]
         cols = pl.ds(pl.multiple_of(g * E, E), E)
         at = lax.broadcasted_iota(jnp.int32, (ROWS, E), 0)
         ots[:, cols] = jnp.where(at == idx[k, g, 0:1, :], 1.0, 0.0).astype(BF16)
@@ -289,7 +325,7 @@
 
     for k in range(2):
         for o in range(GROUPS):
-            prepare(k, order[o])
+            prepare(k, o)
 
             @pl.when(core == 0)
             def _():
@@ -313,6 +349,10 @@
 
             if ch < N_CH - 1:
                 scores(ch)
+        if k == 0:
+            pl.semaphore_wait(relay.at[0], 1)
+            pass_on(1, d, sibling)
+            pl.when(core == 0)(to_down2.start)
         pulls(k)
         for j in range(2):
 
@@ -327,31 +367,28 @@
                 xs[k, span(j)] = dot(q[span(j), :], gt[...], 1, 1).astype(BF16)
 
             x_copy(k, j).start()
-        if k == 0:
-            pl.semaphore_wait(relay.at[0], 1)
-            pass_on(1, d, sibling)
         for j in range(2):
             x_copy(k, j).wait_recv()
         update(k, core, mine)
         if k == 0:
             pl.semaphore_wait(relay.at[1], 1)
-            pl.when(core == 0)(to_down2.start)
             for ch in range(N_CH):
                 for way in range(2):
                     row_copy(1, way, ch).start()
         update(k, 1 - core, other)
 
     to_down.wait_send()
+    across.wait_send()
+    pl.when(jnp.logical_not(first))(down_across.wait_send)
 
     @pl.when(core == 0)
     def _():
-        to_sibling.wait_send()
         to_down2.wait_send()
+        pl.when(first)(onward.wait_send)
 
     @pl.when(core == 1)
     def _():
-        for c in [to_own] + across:
-            c.wait_send()
+        to_own.wait_send()
 
     for k in range(2):
         for j in range(2):
@@ -394,7 +431,6 @@
                 pltpu.VMEM(relation_id.shape, jnp.int32),
                 pltpu.VMEM(negative_row.shape, jnp.int32),
                 pltpu.VMEM((2, 8, E), jnp.int32),
-                pltpu.VMEM((2, 8, E), jnp.int32),
                 pltpu.VMEM((2, GROUPS, 8, E), jnp.int32),
                 pltpu.VMEM((2, 2, 2, COLS, HALF), BF16),
                 pltpu.VMEM((ROWS, COLS), BF16),
@@ -412,11 +448,11 @@
                 dma((2 * N_CH,)),
                 dma((2, 2, N_CH)),
                 dma((2, 2, N_CH)),
-                dma((6,)),
-                dma((6,)),
+                dma((5,)),
+                dma((5,)),
                 dma((2, 2)),
                 dma((2, 2)),
-                pltpu.SemaphoreType.REGULAR((3,)),
+                pltpu.SemaphoreType.REGULAR((4,)),
             ],
             compiler_params=pltpu.CompilerParams(
                 collective_id=0, has_side_effects=True, vmem_limit_bytes=32 * 2**20

time: 39.1 us -> 38.7 us (0.990)
  no operation moved by 1% of the time
where the time goes in v4:
time: 38.7 us; the launch traced here: 38.6 us
  Pallas kernels  37.8 us (98%)
  between operations  0.8 us (2%)
    pallas_call x1, Pallas kernels, body(): pl.pallas_call(functools.partial(kernel, n_dom), out_shape=(pltpu.VMEM((C...  36.8 us
    pallas_call x1, Pallas kernels, body(): pl.pallas_call(write_out, out_shape=(pltpu.HBM((COLS, ROWS), F32), pltpu....  0.94 us

profile of v4, /device:TPU:33, one launch (start us, length us, event | category | flops | bytes accessed | tf_op | source)
XLA Modules:
  0.0 38.6 jit_solution(6530540230282212517)
XLA Ops:
  0.6 36.8 %shard_map.86 = (f32[800,256]{1,0:T(8,128)S(1)}, f32[1,256]{1,0:T(1,128)S(1)}) custom-call(f32[800,256]{1,0:T(8,128)} %bitcast.5, f32[1,256]{1,0:T(1,128)} %bitcast.7, bf16[800,128]{1,0:T(8,128)(2,1)} %bitcast.6, s32[2,1,256]{2,1,0:T(1,128)} %src.1, s32[2,1,256]{2,1,0:T(1,128)} %tgt.1, s32[2,1,256]{2,1,0:T(1,128)} %rid.1, s32[2,1,1,1024]{3,2,1,0:T(1,128)} %neg.1), custom_call_target="tpu_custom_call" | custom-call | tf_op jit(solution)/shard_map/pallas_call | solution.py:420
  37.5 0.9 %shard_map.87 = (f32[800,256]{1,0:T(8,128)}, f32[1,256]{1,0:T(1,128)}) custom-call(f32[800,256]{1,0:T(8,128)S(1)} %get-tuple-element.6.w, f32[1,256]{1,0:T(1,128)S(1)} %get-tuple-element.7.s), custom_call_target="tpu_custom_call" | custom-call | tf_op jit(solution)/shard_map/pallas_call | solution.py:474

commit v5 on v4

--- a/solution.py
+++ b/solution.py
@@ -311,16 +311,17 @@
             gs[re, cols] = gq[:n] * rr + gq[n:] * ri
             gs[im, cols] = gq[n:] * rr - gq[:n] * ri
 
+    def squares(k, j):
+        g = xs[k, span(j)].astype(F32) + xr[k, span(j)].astype(F32)
+        return jnp.sum(g * g, axis=0, keepdims=True)
+
     def update(k, half, lane):
         g = xs[k, :, lane].astype(F32) + xr[k, :, lane].astype(F32)
-        new_s = statev[:, lane] + jnp.sum(g * g, axis=0, keepdims=True) * (1.0 / COLS)
-        new_w = w[:, lane] - g * (learning_rate * lax.rsqrt(new_s))
+        new_w = w[:, lane] - g * (learning_rate * lax.rsqrt(statev[:, lane]))
         if k == 0:
-            statev[:, lane] = new_s
             w[:, lane] = new_w
             buf[1, core, half] = new_w.astype(BF16)
         else:
-            out_s[:, lane] = new_s
             out_w[:, lane] = new_w
 
     for k in range(2):
@@ -367,8 +368,13 @@
                 xs[k, span(j)] = dot(q[span(j), :], gt[...], 1, 1).astype(BF16)
 
             x_copy(k, j).start()
+        total = jnp.zeros((1, ROWS), F32)
         for j in range(2):
             x_copy(k, j).wait_recv()
+            total += squares(k, j)
+        statev[...] = statev[...] + total * (1.0 / COLS)
+        if k == 1:
+            out_s[...] = statev[...]
         update(k, core, mine)
         if k == 0:
             pl.semaphore_wait(relay.at[1], 1)

time: 38.7 us -> 38.8 us (level)
  no operation moved by 1% of the time
where the time goes in v5:
time: 38.8 us; the launch traced here: 38.6 us
  Pallas kernels  37.8 us (97%)
  between operations  0.8 us (2%)
    pallas_call x1, Pallas kernels, body(): pl.pallas_call(functools.partial(kernel, n_dom), out_shape=(pltpu.VMEM((C...  36.9 us
    pallas_call x1, Pallas kernels, body(): pl.pallas_call(write_out, out_shape=(pltpu.HBM((COLS, ROWS), F32), pltpu....  0.94 us

profile of v5, /device:TPU:33, one launch (start us, length us, event | category | flops | bytes accessed | tf_op | source)
XLA Modules:
  0.0 38.6 jit_solution(12387746215382195971)
XLA Ops:
  0.6 36.9 %shard_map.86 = (f32[800,256]{1,0:T(8,128)S(1)}, f32[1,256]{1,0:T(1,128)S(1)}) custom-call(f32[800,256]{1,0:T(8,128)} %bitcast.5, f32[1,256]{1,0:T(1,128)} %bitcast.7, bf16[800,128]{1,0:T(8,128)(2,1)} %bitcast.6, s32[2,1,256]{2,1,0:T(1,128)} %src.1, s32[2,1,256]{2,1,0:T(1,128)} %tgt.1, s32[2,1,256]{2,1,0:T(1,128)} %rid.1, s32[2,1,1,1024]{3,2,1,0:T(1,128)} %neg.1), custom_call_target="tpu_custom_call" | custom-call | tf_op jit(solution)/shard_map/pallas_call | solution.py:426
  37.5 0.9 %shard_map.87 = (f32[800,256]{1,0:T(8,128)}, f32[1,256]{1,0:T(1,128)}) custom-call(f32[800,256]{1,0:T(8,128)S(1)} %get-tuple-element.6.w, f32[1,256]{1,0:T(1,128)S(1)} %get-tuple-element.7.s), custom_call_target="tpu_custom_call" | custom-call | tf_op jit(solution)/shard_map/pallas_call | solution.py:480
